TPU v7x, 128 devices: a whole 4x4x4 slice. The times are simulated.
128 devices in a mesh: row: 8 (over x, core), col: 16 (over z, y).
Axes of the slice: x: 4, y: 4, z: 4, core: 2. Of those that a mesh axis runs over, the one named last changes fastest.
Arguments:
- density: bfloat16 [6144, 6144], P('row', 'col'), may hold values from -5 to 5
- strips: bfloat16 [16384, 8, 128], P(('row', 'col')), may hold values from -5 to 5
- dest_device: int32 [16384, 1], P(('row', 'col')), may hold values from 0 to 127; in each aligned block of 128 rows (0 to 127, 128 to 255, ...) at most 2 rows name the same one
- atom_slot: int32 [16384], P(('row', 'col')), may hold values from 0 to 95
- block_slot: int32 [16384], P(('row', 'col')), may hold values from 0 to 2
- patterns: int32 [3, 48, 48], replicated, may hold values 0 or 1
Outputs:
- density_next: float32 [6144, 6144], P('row', 'col')
- response_next: float32 [6144, 6144], P('row', 'col')
Inputs may be any that keep to these rules, and one draw needn't show every extreme that they name: `dest_device`: of the 128 strips of one device, at most 2 name the same owner, and some owner is named that often.
All inputs are finite; a program needn't handle non-finite values.
Results may differ from a plain program's by a relative error of at most 0.0036.
Values may be sent and summed in bfloat16 or wider, within the bound.
A program may use at most 128 MiB of HBM per device.

v0:
```python
import math
import jax
import jax.numpy as jnp
from jax import lax
from jax.sharding import PartitionSpec as P

STEPS = 2
CAPACITY = 2


def tile_kept(patterns, which, row_offset, col_offset, block_rows, block_cols, block_width):
    window = lax.dynamic_slice(patterns[which], (row_offset, col_offset), (block_rows, block_cols))
    global_rows = row_offset + lax.iota(jnp.int32, block_rows)
    global_cols = col_offset + lax.iota(jnp.int32, block_cols)
    diagonal = (global_rows[:, None] == global_cols[None, :]).astype(jnp.int32)
    kept = jnp.maximum(window, diagonal).astype(jnp.float32)
    return jnp.repeat(jnp.repeat(kept, block_width, axis=0), block_width, axis=1)


def products(zeroth, linear):
    col_zero, col_first = (
        lax.all_gather(zeroth, "row", axis=0, tiled=True),
        lax.all_gather(linear, "row", axis=0, tiled=True),
    )
    pieces = (
        lax.all_gather(zeroth, "col", axis=1, tiled=True),
        lax.all_gather(linear, "col", axis=1, tiled=True),
    )
    square = jnp.dot(pieces[0], col_zero, preferred_element_type=jnp.float32)
    left_part = jnp.dot(pieces[0], col_first, preferred_element_type=jnp.float32)
    right_part = jnp.dot(pieces[1], col_zero, preferred_element_type=jnp.float32)
    return (square, left_part + right_part)


def on_device(density, strips, dest_device, atom_slot, block_slot, patterns):
    tile_rows, tile_cols = density.shape
    mesh_rows = lax.axis_size("row")
    mesh_cols = lax.axis_size("col")
    devices = mesh_rows * mesh_cols
    matrix_order = tile_rows * mesh_rows
    atom_width = strips.shape[1]
    block_width = strips.shape[2]
    block_rows = tile_rows // block_width
    block_cols = tile_cols // block_width
    row_offset = lax.axis_index("row") * block_rows
    col_offset = lax.axis_index("col") * block_cols
    kept_zero = tile_kept(patterns, 0, row_offset, col_offset, block_rows, block_cols, block_width)
    kept_first = tile_kept(patterns, 1, row_offset, col_offset, block_rows, block_cols, block_width)
    kept_field = tile_kept(patterns, 2, row_offset, col_offset, block_rows, block_cols, block_width)
    capacity = CAPACITY
    targets = dest_device[:, 0]
    matches = (targets[:, None] == lax.iota(jnp.int32, devices)[None, :]).astype(jnp.int32)
    before = jnp.cumsum(matches, axis=0) - matches
    ranking = jnp.sum(before * matches, axis=1)
    position = targets * capacity + ranking
    sent_strips = (
        jnp.zeros((devices * capacity, atom_width, block_width), strips.dtype)
        .at[position]
        .set(strips)
    )
    sent_atoms = jnp.full((devices * capacity,), -1, jnp.int32).at[position].set(atom_slot)
    sent_blocks = jnp.zeros((devices * capacity,), jnp.int32).at[position].set(block_slot)
    arrived = (
        lax.all_to_all(
            sent_strips.reshape(devices, capacity, atom_width, block_width),
            ("row", "col"),
            split_axis=0,
            concat_axis=0,
            tiled=True,
        ),
        lax.all_to_all(
            sent_atoms.reshape(devices, capacity),
            ("row", "col"),
            split_axis=0,
            concat_axis=0,
            tiled=True,
        ),
        lax.all_to_all(
            sent_blocks.reshape(devices, capacity),
            ("row", "col"),
            split_axis=0,
            concat_axis=0,
            tiled=True,
        ),
    )
    recv_strips = arrived[0].reshape(-1, atom_width * block_width)
    recv_atoms = arrived[1].reshape(-1)
    recv_blocks = arrived[2].reshape(-1)
    atoms_here = tile_rows // atom_width
    atom_match = recv_atoms[:, None] == lax.iota(jnp.int32, atoms_here)[None, :]
    block_match = recv_blocks[:, None] == lax.iota(jnp.int32, block_cols)[None, :]
    placing = (
        (atom_match[:, :, None] & block_match[:, None, :])
        .astype(jnp.bfloat16)
        .reshape(-1, atoms_here * block_cols)
    )
    summed = lax.dot_general(
        placing, recv_strips, (((0,), (0,)), ((), ())), preferred_element_type=jnp.float32
    )
    h_field = (
        summed.reshape(atoms_here, block_cols, atom_width, block_width)
        .transpose(0, 2, 1, 3)
        .reshape(tile_rows, tile_cols)
    )
    linear = (-(kept_field * h_field)).astype(jnp.bfloat16)
    zeroth = density
    inv_root = 1.0 / math.sqrt(matrix_order)
    new_zeroth = None
    new_linear = None
    for iteration in range(STEPS):
        square, crossed = products(zeroth, linear)
        if iteration % 2 == 0:
            new_zeroth = kept_zero * (square * inv_root)
            new_linear = kept_first * (crossed * inv_root)
        else:
            new_zeroth = kept_zero * (2.0 * zeroth.astype(jnp.float32) - square * inv_root)
            new_linear = kept_first * (2.0 * linear.astype(jnp.float32) - crossed * inv_root)
        zeroth = new_zeroth.astype(jnp.bfloat16)
        linear = new_linear.astype(jnp.bfloat16)
    return (new_zeroth, new_linear)


def solution(mesh):
    return jax.shard_map(
        on_device,
        mesh=mesh,
        in_specs=(
            P("row", "col"),
            P(("row", "col"), None, None),
            P(("row", "col"), None),
            P(("row", "col")),
            P(("row", "col")),
            P(),
        ),
        out_specs=(P("row", "col"), P("row", "col")),
        check_vma=False,
    )
```

profile of v0, /device:TPU:0, one launch (start us, length us, event | category | flops | bytes accessed | tf_op | source)
XLA Modules:
  0.0 541.6 jit_solution(12071236785653305353)
XLA Ops:
  7.2 0.7 all-gather.11.cloned.1.call-update
  7.9 0.7 fusion.14
  8.7 0.2 reduce_window_sum.11
  8.8 0.8 select_reduce_fusion
  9.7 0.7 fusion.18
  10.3 1.1 scatter_custom_fusion.1
  11.4 0.8 all_to_all.17
  12.2 11.1 %all-to-all-start.1 = ((s32[128,1,2]{2,1,0:T(1,128)}), s32[128,1,2]{2,1,0:T(1,128)S(1)}, u32[]{:S(2)}, u32[]{:S(2)}) async-start(s32[128,1,2]{2,1,0:T(1,128)} %bitcast.10), calls=%async_computation.1 | async-start | bytes 131072 | tf_op jit(solution)/shard_map/all_to_all | solution.py:78
  23.4 0.8 fusion.23
  24.7 1.1 scatter_custom_fusion
  25.8 0.8 all_to_all.15
  26.6 6.2 %all-to-all-done.1 = s32[128,1,2]{2,1,0:T(1,128)S(1)} async-done(((s32[128,1,2]{2,1,0:T(1,128)}), s32[128,1,2]{2,1,0:T(1,128)S(1)}, u32[]{:S(2)}, u32[]{:S(2)}) %all-to-all-start.1) | async-done | bytes 1056 | tf_op jit(solution)/shard_map/all_to_all | solution.py:78
  32.8 4.6 all-to-all-start
  37.5 0.9 broadcast_in_dim.49
  38.3 13.3 %scatter_fusion = bf16[256,8,128]{2,1,0:T(8,128)(2,1)} fusion(bf16[256,8,128]{2,1,0:T(8,128)(2,1)} %broadcast_in_dim.49, s32[128]{0:T(128)S(1)} %fusion.18, bf16[128,8,128]{2,1,0:T(8,128)(2,1)S(1)} %copy-done.2), kind=kCustom, calls=%fused_computation.2 | custom fusion | bytes 786944 | tf_op jit(solution)/shard_map/scatter | solution.py:59
  51.6 0.6 broadcast.69
  52.2 0.8 reduce.6
  53.1 0.1 eq.91
  53.2 9.8 %all-to-all-start.2 = ((bf16[128,2,8,128]{3,2,1,0:T(8,128)(2,1)}), bf16[128,2,8,128]{3,2,1,0:T(8,128)(2,1)S(1)}, u32[]{:S(2)}, u32[]{:S(2)}) async-start(bf16[128,2,8,128]{3,2,1,0:T(8,128)(2,1)} %bitcast.13), calls=%async_computation.2 | async-start | bytes 1048576 | tf_op jit(solution)/shard_map/all_to_all | solution.py:64
  63.1 0.8 reduce.7
  63.9 0.1 eq.87
  64.2 0.1 and.22
  64.5 12.2 %all-to-all-done.2 = bf16[128,2,8,128]{3,2,1,0:T(8,128)(2,1)S(1)} async-done(((bf16[128,2,8,128]{3,2,1,0:T(8,128)(2,1)}), bf16[128,2,8,128]{3,2,1,0:T(8,128)(2,1)S(1)}, u32[]{:S(2)}, u32[]{:S(2)}) %all-to-all-start.2) | async-done | bytes 524320 | tf_op jit(solution)/shard_map/all_to_all | solution.py:64
  76.7 0.2 copy.34
  76.9 0.4 convolution_bitcast_fusion.1
  77.3 0.7 copy.56
  78.0 0.4 copy.37
  78.4 0.9 fusion.12
  79.3 0.7 all-gather.17.cloned.1.call-update
  80.1 0.5 all-gather.9.cloned.1.call-update
  80.8 0.4 copy.40
  81.2 69.7 %all-gather.19.cloned.1.call-done = bf16[768,6144]{0,1:T(8,128)(2,1)} async-done(((bf16[768,384]{0,1:T(8,128)(2,1)}), bf16[768,6144]{0,1:T(8,128)(2,1)}) %all-gather.19.cloned.1.call-update) | async-done | bytes 9437200 | tf_op jit(solution)/shard_map/all_gather | solution.py:27
  150.9 9.0 %fusion.24 = f32[768,384]{1,0:T(8,128)S(1)} fusion(bf16[768,6144]{0,1:T(8,128)(2,1)} %all-gather.19.cloned.1.call-done, bf16[6144,384]{1,0:T(8,128)(2,1)} %all-gather.11.cloned.1.call-done), kind=kOutput, calls=%fused_computation.56 | convolution fusion | flops 3623878656 | bytes 15335424 | tf_op jit(solution)/shard_map/dot_general | solution.py:31
  159.9 27.1 %all-gather.17.cloned.1.call-done = bf16[6144,384]{0,1:T(8,128)(2,1)} async-done(((bf16[768,384]{0,1:T(8,128)(2,1)}), bf16[6144,384]{0,1:T(8,128)(2,1)}) %all-gather.17.cloned.1.call-update) | async-done | bytes 4718608 | tf_op jit(solution)/shard_map/all_gather | solution.py:23
  187.1 85.9 %all-gather.9.cloned.1.call-done = bf16[768,6144]{1,0:T(8,128)(2,1)} async-done(((bf16[768,384]{1,0:T(8,128)(2,1)}), bf16[768,6144]{1,0:T(8,128)(2,1)}) %all-gather.9.cloned.1.call-update) | async-done | bytes 9437200 | tf_op jit(solution)/shard_map/all_gather | solution.py:26
  272.9 9.8 %fusion.9 = bf16[768,384]{1,0:T(8,128)(2,1)} fusion(f32[768,384]{1,0:T(8,128)S(1)} %copy.40, f32[768,384]{1,0:T(8,128)S(1)} %fusion.24, bf16[6144,384]{0,1:T(8,128)(2,1)} %all-gather.17.cloned.1.call-done, bf16[768,6144]{1,0:T(8,128)(2,1)} %all-gather.9.cloned.1.call-done), kind=kOutput, calls=%fused_computation.17 | convolution fusion | flops 3625058304 | bytes 17104896 | tf_op jit(solution)/shard_map/dot_general | solution.py:30
  282.8 0.2 all-gather.13.cloned.1.call-start
  283.2 0.4 copy.29
  283.5 9.7 %fusion.10 = bf16[768,384]{1,0:T(8,128)(2,1)} fusion(f32[768,384]{1,0:T(8,128)S(1)} %copy.29, bf16[768,6144]{1,0:T(8,128)(2,1)} %all-gather.9.cloned.1.call-done, bf16[6144,384]{1,0:T(8,128)(2,1)} %all-gather.11.cloned.1.call-done), kind=kOutput, calls=%fused_computation.18 | convolution fusion | flops 3624763392 | bytes 15925248 | tf_op jit(solution)/shard_map/dot_general | solution.py:29
  293.3 0.7 all-gather.15.cloned.1.call-update
  294.1 0.7 all-gather.23.cloned.1.call-update
  294.8 21.6 %all-gather.21.cloned.1.call-done = bf16[6144,384]{1,0:T(8,128)(2,1)} async-done(((bf16[768,384]{1,0:T(8,128)(2,1)}), bf16[6144,384]{1,0:T(8,128)(2,1)}) %all-gather.21.cloned.1.call-update) | async-done | bytes 4718608 | tf_op jit(solution)/shard_map/all_gather | solution.py:23
  316.4 86.4 %all-gather.13.cloned.1.call-done = bf16[768,6144]{1,0:T(8,128)(2,1)} async-done(((bf16[768,384]{1,0:T(8,128)(2,1)}), bf16[768,6144]{1,0:T(8,128)(2,1)}) %all-gather.13.cloned.1.call-update) | async-done | bytes 9437200 | tf_op jit(solution)/shard_map/all_gather | solution.py:26
  402.9 9.8 %fusion.25 = f32[768,384]{1,0:T(8,128)} fusion(bf16[768,6144]{1,0:T(8,128)(2,1)} %all-gather.13.cloned.1.call-done, bf16[6144,384]{1,0:T(8,128)(2,1)} %all-gather.21.cloned.1.call-done), kind=kOutput, calls=%fused_computation.57 | convolution fusion | flops 3623878656 | bytes 15335424 | tf_op jit(solution)/shard_map/dot_general | solution.py:30
  412.6 26.0 %all-gather.15.cloned.1.call-done = bf16[6144,384]{1,0:T(8,128)(2,1)} async-done(((bf16[768,384]{1,0:T(8,128)(2,1)}), bf16[6144,384]{1,0:T(8,128)(2,1)}) %all-gather.15.cloned.1.call-update) | async-done | bytes 4718608 | tf_op jit(solution)/shard_map/all_gather | solution.py:22
  438.7 9.8 %fusion.2 = f32[768,384]{1,0:T(8,128)} fusion(f32[768,384]{1,0:T(8,128)S(1)} %copy.29, bf16[768,6144]{1,0:T(8,128)(2,1)} %all-gather.13.cloned.1.call-done, bf16[6144,384]{1,0:T(8,128)(2,1)} %all-gather.15.cloned.1.call-done, bf16[768,384]{1,0:T(8,128)(2,1)S(1)} %copy-done.1), kind=kOutput, calls=%fused_computation.9 | convolution fusion | flops 3625353216 | bytes 17104896 | tf_op jit(solution)/shard_map/dot_general | solution.py:29
  448.5 76.2 %all-gather.23.cloned.1.call-done = bf16[768,6144]{1,0:T(8,128)(2,1)} async-done(((bf16[768,384]{1,0:T(8,128)(2,1)}), bf16[768,6144]{1,0:T(8,128)(2,1)}) %all-gather.23.cloned.1.call-update) | async-done | bytes 9437200 | tf_op jit(solution)/shard_map/all_gather | solution.py:27
  524.7 10.1 %fusion.8 = f32[768,384]{1,0:T(8,128)} fusion(f32[768,384]{1,0:T(8,128)S(1)} %copy.40, f32[768,384]{1,0:T(8,128)} %fusion.25, bf16[768,6144]{1,0:T(8,128)(2,1)} %all-gather.23.cloned.1.call-done, bf16[6144,384]{1,0:T(8,128)(2,1)} %all-gather.15.cloned.1.call-done, bf16[768,384]{1,0:T(8,128)(2,1)S(1)} %copy-done), kind=kOutput, calls=%fused_computation.16 | convolution fusion | flops 3625648128 | bytes 18284544 | tf_op jit(solution)/shard_map/dot_general | solution.py:31
  (39 shorter events, 1.6 us)
Async XLA Ops:
  7.2 31.2 %copy-start.2 = (bf16[128,8,128]{2,1,0:T(8,128)(2,1)S(1)}, bf16[128,8,128]{2,1,0:T(8,128)(2,1)}, u32[]{:S(2)}) copy-start(bf16[128,8,128]{2,1,0:T(8,128)(2,1)} %param.7) | copy-start | bytes 786436
  7.2 74.1 %all-gather.11.cloned.1.call-start = ((), (), s32[]{:S(2)}) async-start(), calls=%async_computation.4 | async-start | bytes 5308416 | tf_op jit(solution)/shard_map/all_gather | solution.py:22
  12.2 20.6 %all-to-all-start.1 = ((s32[128,1,2]{2,1,0:T(1,128)}), s32[128,1,2]{2,1,0:T(1,128)S(1)}, u32[]{:S(2)}, u32[]{:S(2)}) async-start(s32[128,1,2]{2,1,0:T(1,128)} %bitcast.10), calls=%async_computation.1 | async-start | bytes 131072 | tf_op jit(solution)/shard_map/all_to_all | solution.py:78
  32.8 20.5 %all-to-all-start = ((s32[128,1,2]{2,1,0:T(1,128)}), s32[128,1,2]{2,1,0:T(1,128)S(1)}, u32[]{:S(2)}, u32[]{:S(2)}) async-start(s32[128,1,2]{2,1,0:T(1,128)} %bitcast.9), calls=%async_computation | async-start | bytes 131072 | tf_op jit(solution)/shard_map/all_to_all | solution.py:71
  53.2 23.4 %all-to-all-start.2 = ((bf16[128,2,8,128]{3,2,1,0:T(8,128)(2,1)}), bf16[128,2,8,128]{3,2,1,0:T(8,128)(2,1)S(1)}, u32[]{:S(2)}, u32[]{:S(2)}) async-start(bf16[128,2,8,128]{3,2,1,0:T(8,128)(2,1)} %bitcast.13), calls=%async_computation.2 | async-start | bytes 1048576 | tf_op jit(solution)/shard_map/all_to_all | solution.py:64
  63.0 87.9 %all-gather.19.cloned.1.call-start = ((), (), s32[]{:S(2)}) async-start(), calls=%async_computation.8 | async-start | bytes 10027008 | tf_op jit(solution)/shard_map/all_gather | solution.py:27
  79.3 107.8 %all-gather.17.cloned.1.call-start = ((), (), s32[]{:S(2)}) async-start(), calls=%async_computation.7 | async-start | bytes 5308416 | tf_op jit(solution)/shard_map/all_gather | solution.py:23
  80.0 192.9 %all-gather.9.cloned.1.call-start = ((), (), s32[]{:S(2)}) async-start(), calls=%async_computation.3 | async-start | bytes 10027008 | tf_op jit(solution)/shard_map/all_gather | solution.py:26
  80.6 235.8 %all-gather.21.cloned.1.call-start = ((), (), s32[]{:S(2)}) async-start(), calls=%async_computation.9 | async-start | bytes 5308416 | tf_op jit(solution)/shard_map/all_gather | solution.py:23
  282.8 120.1 %all-gather.13.cloned.1.call-start = ((), (), s32[]{:S(2)}) async-start(), calls=%async_computation.5 | async-start | bytes 10027008 | tf_op jit(solution)/shard_map/all_gather | solution.py:26
  293.3 145.4 %all-gather.15.cloned.1.call-start = ((), (), s32[]{:S(2)}) async-start(), calls=%async_computation.6 | async-start | bytes 5308416 | tf_op jit(solution)/shard_map/all_gather | solution.py:22
  294.0 230.6 %all-gather.23.cloned.1.call-start = ((), (), s32[]{:S(2)}) async-start(), calls=%async_computation.10 | async-start | bytes 10027008 | tf_op jit(solution)/shard_map/all_gather | solution.py:27
  294.8 143.9 %copy-start.1 = (bf16[768,384]{1,0:T(8,128)(2,1)S(1)}, bf16[768,384]{1,0:T(8,128)(2,1)}, u32[]{:S(2)}) copy-start(bf16[768,384]{1,0:T(8,128)(2,1)} %fusion.10) | copy-start | bytes 1769476
  412.6 112.0 %copy-start = (bf16[768,384]{1,0:T(8,128)(2,1)S(1)}, bf16[768,384]{1,0:T(8,128)(2,1)}, u32[]{:S(2)}) copy-start(bf16[768,384]{1,0:T(8,128)(2,1)} %fusion.9) | copy-start | bytes 1769476
Sparse Core Ops, SparseCore 0:
  9.7 38.0 all-gather.10
  79.4 71.4 all-gather.18
  153.2 33.8 all-gather.16
  189.0 83.8 all-gather.8
  282.9 33.4 all-gather.20
  319.0 83.8 all-gather.12
  405.1 33.4 all-gather.14
  440.8 83.8 all-gather.22
where the time goes:
time: 542 us
  waiting for transfers between devices  415 us (77%)
  matrix products  58.5 us (11%)
  starting transfers between devices  26 us (5%)
  local copies, waits for them, and re-layouts  22.7 us (4%)
  between operations  14.4 us (3%)
    all_gather x2, waiting for transfers between devices, products(): lax.all_gather(zeroth, 'col', axis=1, tiled=True)  172 us
    all_gather x2, waiting for transfers between devices, products(): lax.all_gather(linear, 'col', axis=1, tiled=True)  146 us
    all_gather x2, waiting for transfers between devices, products(): lax.all_gather(linear, 'row', axis=0, tiled=True)  48.8 us
    all_gather x2, waiting for transfers between devices, products(): lax.all_gather(zeroth, 'row', axis=0, tiled=True)  26 us
    dot_general x2, matrix products, products(): jnp.dot(pieces[0], col_first, preferred_element_type=jnp.float32)  19.6 us
    dot_general x2, matrix products, products(): square = jnp.dot(pieces[0], col_zero, preferred_element_type=jnp.float32)  19.5 us
    dot_general x2, matrix products, products(): jnp.dot(pieces[1], col_zero, preferred_element_type=jnp.float32)  19.1 us
    scatter x1, local copies, waits for them, and re-layouts, on_device(): sent_strips = jnp.zeros((devices * capacity, atom_width, block_width), st...  13.3 us
  transfers between devices with their start and end apart: 11, of which 9 were waited for; matrix products, arithmetic and copies ran while one was open for 12% of the time, Pallas kernels for 0%

commit v1 on v0

--- a/solution.py
+++ b/solution.py
@@ -18,8 +18,17 @@
 
 
 def products(zeroth, linear):
+    set_rates = lambda body, lane_axis: jnp.concatenate(
+        lax.all_to_all(
+            jnp.stack([body for _ in range(lax.psum(1, axis_name=lane_axis))]),
+            axis_name=lane_axis,
+            split_axis=0,
+            concat_axis=0,
+        ),
+        axis=0,
+    )
     col_zero, col_first = (
-        lax.all_gather(zeroth, "row", axis=0, tiled=True),
+        set_rates(zeroth, "row"),
         lax.all_gather(linear, "row", axis=0, tiled=True),
     )
     pieces = (

time: 542 us -> 522 us (0.963)
  waiting for transfers between devices: 415 us -> 379 us
  starting transfers between devices: 26 us -> 35.4 us
    all_gather x2, waiting for transfers between devices: 146 us -> 72.6 us  [products(): lax.all_gather(linear, 'col', axis=1, tiled=True)]
    all_to_all x0 -> x2, waiting for transfers between devices: none -> 54.5 us  [products(): lax.all_to_all(jnp.stack([body for _ in range(lax.psum(1, axis_name=lane_...]
    all_gather x2 -> x0, waiting for transfers between devices: 26 us -> none  [products(): lax.all_gather(zeroth, 'row', axis=0, tiled=True)]
    all_to_all x0 -> x2, starting transfers between devices: none -> 9.46 us  [products(): lax.all_to_all(jnp.stack([body for _ in range(lax.psum(1, axis_name=lane_...]
    all_gather x2, waiting for transfers between devices: 48.8 us -> 57.6 us  [products(): lax.all_gather(linear, 'row', axis=0, tiled=True)]
where the time goes in v1:
time: 522 us; the launch traced here: 521 us
  waiting for transfers between devices  379 us (73%)
  matrix products  59.1 us (11%)
  starting transfers between devices  35.4 us (7%)
  local copies, waits for them, and re-layouts  28.1 us (5%)
  between operations  14.4 us (3%)
    all_gather x2, waiting for transfers between devices, products(): lax.all_gather(zeroth, 'col', axis=1, tiled=True)  174 us
    all_gather x2, waiting for transfers between devices, products(): lax.all_gather(linear, 'col', axis=1, tiled=True)  72.6 us
    all_gather x2, waiting for transfers between devices, products(): lax.all_gather(linear, 'row', axis=0, tiled=True)  57.6 us
    all_to_all x2, waiting for transfers between devices, products(): lax.all_to_all(jnp.stack([body for _ in range(lax.psum(1, axis_name=lane_...  54.5 us
    dot_general x2, matrix products, products(): square = jnp.dot(pieces[0], col_zero, preferred_element_type=jnp.float32)  20.1 us
    dot_general x2, matrix products, products(): jnp.dot(pieces[0], col_first, preferred_element_type=jnp.float32)  19.6 us
    dot_general x2, matrix products, products(): jnp.dot(pieces[1], col_zero, preferred_element_type=jnp.float32)  19.1 us
    scatter x1, local copies, waits for them, and re-layouts, on_device(): sent_strips = jnp.zeros((devices * capacity, atom_width, block_width), st...  13.3 us
  transfers between devices with their start and end apart: 11, of which 9 were waited for; matrix products, arithmetic and copies ran while one was open for 12% of the time, Pallas kernels for 0%

profile of v1, /device:TPU:0, one launch (start us, length us, event | category | flops | bytes accessed | tf_op | source)
XLA Modules:
  0.0 521.2 jit_solution(15566777242646159375)
XLA Ops:
  7.2 0.8 fusion.14
  8.0 0.2 reduce_window_sum.11
  8.1 0.8 select_reduce_fusion
  9.0 0.7 fusion.18
  9.6 1.1 scatter_custom_fusion.1
  10.7 0.8 all_to_all.25
  11.5 11.1 %all-to-all-start.3 = ((s32[128,1,2]{2,1,0:T(1,128)}), s32[128,1,2]{2,1,0:T(1,128)S(1)}, u32[]{:S(2)}, u32[]{:S(2)}) async-start(s32[128,1,2]{2,1,0:T(1,128)} %bitcast.12), calls=%async_computation.3 | async-start | bytes 131072 | tf_op jit(solution)/shard_map/all_to_all | solution.py:87
  22.7 0.8 fusion.23
  24.0 1.1 scatter_custom_fusion
  25.1 0.8 all_to_all.23
  25.9 6.2 %all-to-all-done.3 = s32[128,1,2]{2,1,0:T(1,128)S(1)} async-done(((s32[128,1,2]{2,1,0:T(1,128)}), s32[128,1,2]{2,1,0:T(1,128)S(1)}, u32[]{:S(2)}, u32[]{:S(2)}) %all-to-all-start.3) | async-done | bytes 1056 | tf_op jit(solution)/shard_map/all_to_all | solution.py:87
  32.1 4.6 all-to-all-start.2
  36.8 0.9 broadcast_in_dim.49
  37.6 13.3 %scatter_fusion = bf16[256,8,128]{2,1,0:T(8,128)(2,1)} fusion(bf16[256,8,128]{2,1,0:T(8,128)(2,1)} %broadcast_in_dim.49, s32[128]{0:T(128)S(1)} %fusion.18, bf16[128,8,128]{2,1,0:T(8,128)(2,1)S(1)} %copy-done.3), kind=kCustom, calls=%fused_computation.2 | custom fusion | bytes 786944 | tf_op jit(solution)/shard_map/scatter | solution.py:68
  50.9 0.5 broadcast.73
  51.4 0.7 reduce.6
  52.3 9.8 %all-to-all-start.4 = ((bf16[128,2,8,128]{3,2,1,0:T(8,128)(2,1)}), bf16[128,2,8,128]{3,2,1,0:T(8,128)(2,1)S(1)}, u32[]{:S(2)}, u32[]{:S(2)}) async-start(bf16[128,2,8,128]{3,2,1,0:T(8,128)(2,1)} %bitcast.15), calls=%async_computation.4 | async-start | bytes 1048576 | tf_op jit(solution)/shard_map/all_to_all | solution.py:73
  62.1 0.7 reduce.7
  63.4 12.3 %all-to-all-done.4 = bf16[128,2,8,128]{3,2,1,0:T(8,128)(2,1)S(1)} async-done(((bf16[128,2,8,128]{3,2,1,0:T(8,128)(2,1)}), bf16[128,2,8,128]{3,2,1,0:T(8,128)(2,1)S(1)}, u32[]{:S(2)}, u32[]{:S(2)}) %all-to-all-start.4) | async-done | bytes 524320 | tf_op jit(solution)/shard_map/all_to_all | solution.py:73
  75.8 0.2 copy.34
  76.0 0.4 convolution_bitcast_fusion.1
  76.3 0.7 copy.56
  77.0 0.4 copy.37
  77.4 0.9 fusion.12
  78.4 0.7 all-gather.11.cloned.1.call-update
  79.1 0.7 all-gather.7.cloned.1.call-update
  79.8 2.5 stack.4
  82.4 4.6 all-to-all-start
  87.0 0.2 all-gather.15.cloned.1.call-start
  87.4 0.4 copy.40
  87.8 54.5 %all-to-all-done = bf16[8,768,384]{2,1,0:T(8,128)(2,1)} async-done(((bf16[8,768,384]{2,1,0:T(8,128)(2,1)}), bf16[8,768,384]{2,1,0:T(8,128)(2,1)}, u32[]{:S(2)}, u32[]{:S(2)}) %all-to-all-start) | async-done | bytes 4718624 | tf_op jit(solution)/shard_map/all_to_all | solution.py:22
  142.3 7.7 %all-gather.13.cloned.1.call-done = bf16[768,6144]{0,1:T(8,128)(2,1)} async-done(((bf16[768,384]{0,1:T(8,128)(2,1)}), bf16[768,6144]{0,1:T(8,128)(2,1)}) %all-gather.13.cloned.1.call-update) | async-done | bytes 9437200 | tf_op jit(solution)/shard_map/all_gather | solution.py:36
  150.0 9.0 %fusion.24 = f32[768,384]{1,0:T(8,128)S(1)} fusion(bf16[768,6144]{0,1:T(8,128)(2,1)} %all-gather.13.cloned.1.call-done, bf16[6144,384]{1,0:T(8,128)(2,1)} %bitcast.2), kind=kOutput, calls=%fused_computation.56 | convolution fusion | flops 3623878656 | bytes 15335424 | tf_op jit(solution)/shard_map/dot_general | solution.py:40
  159.0 27.1 %all-gather.11.cloned.1.call-done = bf16[6144,384]{0,1:T(8,128)(2,1)} async-done(((bf16[768,384]{0,1:T(8,128)(2,1)}), bf16[6144,384]{0,1:T(8,128)(2,1)}) %all-gather.11.cloned.1.call-update) | async-done | bytes 4718608 | tf_op jit(solution)/shard_map/all_gather | solution.py:32
  186.1 86.0 %all-gather.7.cloned.1.call-done = bf16[768,6144]{1,0:T(8,128)(2,1)} async-done(((bf16[768,384]{1,0:T(8,128)(2,1)}), bf16[768,6144]{1,0:T(8,128)(2,1)}) %all-gather.7.cloned.1.call-update) | async-done | bytes 9437200 | tf_op jit(solution)/shard_map/all_gather | solution.py:35
  272.1 9.8 %fusion.9 = bf16[768,384]{1,0:T(8,128)(2,1)} fusion(f32[768,384]{1,0:T(8,128)S(1)} %copy.40, f32[768,384]{1,0:T(8,128)S(1)} %fusion.24, bf16[6144,384]{0,1:T(8,128)(2,1)} %all-gather.11.cloned.1.call-done, bf16[768,6144]{1,0:T(8,128)(2,1)} %all-gather.7.cloned.1.call-done), kind=kOutput, calls=%fused_computation.17 | convolution fusion | flops 3625058304 | bytes 17104896 | tf_op jit(solution)/shard_map/dot_general | solution.py:39
  282.2 0.4 copy.29
  282.5 9.7 %fusion.10 = bf16[768,384]{1,0:T(8,128)(2,1)} fusion(f32[768,384]{1,0:T(8,128)S(1)} %copy.29, bf16[768,6144]{1,0:T(8,128)(2,1)} %all-gather.7.cloned.1.call-done, bf16[6144,384]{1,0:T(8,128)(2,1)} %bitcast.2), kind=kOutput, calls=%fused_computation.18 | convolution fusion | flops 3624763392 | bytes 15925248 | tf_op jit(solution)/shard_map/dot_general | solution.py:38
  292.3 0.5 all-gather.17.cloned.1.call-update
  292.8 0.5 copy-done.2
  293.3 2.5 stack.5
  295.8 4.8 all-to-all-start.1
  300.7 30.5 %all-gather.15.cloned.1.call-done = bf16[6144,384]{1,0:T(8,128)(2,1)} async-done(((bf16[768,384]{1,0:T(8,128)(2,1)}), bf16[6144,384]{1,0:T(8,128)(2,1)}) %all-gather.15.cloned.1.call-update) | async-done | bytes 4718608 | tf_op jit(solution)/shard_map/all_gather | solution.py:32
  331.1 88.1 %all-gather.9.cloned.1.call-done = bf16[768,6144]{1,0:T(8,128)(2,1)} async-done(((bf16[768,384]{1,0:T(8,128)(2,1)}), bf16[768,6144]{1,0:T(8,128)(2,1)}) %all-gather.9.cloned.1.call-update) | async-done | bytes 9437200 | tf_op jit(solution)/shard_map/all_gather | solution.py:35
  419.2 9.8 %fusion.25 = f32[768,384]{1,0:T(8,128)} fusion(bf16[768,6144]{1,0:T(8,128)(2,1)} %all-gather.9.cloned.1.call-done, bf16[6144,384]{1,0:T(8,128)(2,1)} %all-gather.15.cloned.1.call-done), kind=kOutput, calls=%fused_computation.57 | convolution fusion | flops 3623878656 | bytes 15335424 | tf_op jit(solution)/shard_map/dot_general | solution.py:39
  429.0 10.4 %fusion.2 = f32[768,384]{1,0:T(8,128)} fusion(f32[768,384]{1,0:T(8,128)S(1)} %copy.29, bf16[768,6144]{1,0:T(8,128)(2,1)} %all-gather.9.cloned.1.call-done, bf16[6144,384]{1,0:T(8,128)(2,1)} %bitcast.3, bf16[768,384]{1,0:T(8,128)(2,1)S(1)} %copy-done.2), kind=kOutput, calls=%fused_computation.9 | convolution fusion | flops 3625353216 | bytes 17104896 | tf_op jit(solution)/shard_map/dot_general | solution.py:38
  439.4 64.9 %all-gather.17.cloned.1.call-done = bf16[768,6144]{1,0:T(8,128)(2,1)} async-done(((bf16[768,384]{1,0:T(8,128)(2,1)}), bf16[768,6144]{1,0:T(8,128)(2,1)}) %all-gather.17.cloned.1.call-update) | async-done | bytes 9437200 | tf_op jit(solution)/shard_map/all_gather | solution.py:36
  504.3 10.1 %fusion.8 = f32[768,384]{1,0:T(8,128)} fusion(f32[768,384]{1,0:T(8,128)S(1)} %copy.40, f32[768,384]{1,0:T(8,128)} %fusion.25, bf16[768,6144]{1,0:T(8,128)(2,1)} %all-gather.17.cloned.1.call-done, bf16[6144,384]{1,0:T(8,128)(2,1)} %bitcast.3, bf16[768,384]{1,0:T(8,128)(2,1)S(1)} %copy-done), kind=kOutput, calls=%fused_computation.16 | convolution fusion | flops 3625648128 | bytes 18284544 | tf_op jit(solution)/shard_map/dot_general | solution.py:40
  (41 shorter events, 1.9 us)
Async XLA Ops:
  7.2 30.5 %copy-start.3 = (bf16[128,8,128]{2,1,0:T(8,128)(2,1)S(1)}, bf16[128,8,128]{2,1,0:T(8,128)(2,1)}, u32[]{:S(2)}) copy-start(bf16[128,8,128]{2,1,0:T(8,128)(2,1)} %param.7) | copy-start | bytes 786436
  11.5 20.6 %all-to-all-start.3 = ((s32[128,1,2]{2,1,0:T(1,128)}), s32[128,1,2]{2,1,0:T(1,128)S(1)}, u32[]{:S(2)}, u32[]{:S(2)}) async-start(s32[128,1,2]{2,1,0:T(1,128)} %bitcast.12), calls=%async_computation.3 | async-start | bytes 131072 | tf_op jit(solution)/shard_map/all_to_all | solution.py:87
  32.1 20.2 %all-to-all-start.2 = ((s32[128,1,2]{2,1,0:T(1,128)}), s32[128,1,2]{2,1,0:T(1,128)S(1)}, u32[]{:S(2)}, u32[]{:S(2)}) async-start(s32[128,1,2]{2,1,0:T(1,128)} %bitcast.11), calls=%async_computation.2 | async-start | bytes 131072 | tf_op jit(solution)/shard_map/all_to_all | solution.py:80
  52.3 23.4 %all-to-all-start.4 = ((bf16[128,2,8,128]{3,2,1,0:T(8,128)(2,1)}), bf16[128,2,8,128]{3,2,1,0:T(8,128)(2,1)S(1)}, u32[]{:S(2)}, u32[]{:S(2)}) async-start(bf16[128,2,8,128]{3,2,1,0:T(8,128)(2,1)} %bitcast.15), calls=%async_computation.4 | async-start | bytes 1048576 | tf_op jit(solution)/shard_map/all_to_all | solution.py:73
  62.1 87.9 %all-gather.13.cloned.1.call-start = ((), (), s32[]{:S(2)}) async-start(), calls=%async_computation.8 | async-start | bytes 10027008 | tf_op jit(solution)/shard_map/all_gather | solution.py:36
  78.3 1.5 copy-start.1
  78.3 107.8 %all-gather.11.cloned.1.call-start = ((), (), s32[]{:S(2)}) async-start(), calls=%async_computation.7 | async-start | bytes 5308416 | tf_op jit(solution)/shard_map/all_gather | solution.py:32
  79.1 193.0 %all-gather.7.cloned.1.call-start = ((), (), s32[]{:S(2)}) async-start(), calls=%async_computation.5 | async-start | bytes 10027008 | tf_op jit(solution)/shard_map/all_gather | solution.py:35
  82.4 59.9 %all-to-all-start = ((bf16[8,768,384]{2,1,0:T(8,128)(2,1)}), bf16[8,768,384]{2,1,0:T(8,128)(2,1)}, u32[]{:S(2)}, u32[]{:S(2)}) async-start(bf16[8,768,384]{2,1,0:T(8,128)(2,1)} %stack.4), calls=%async_computation | async-start | bytes 9437184 | tf_op jit(solution)/shard_map/all_to_all | solution.py:22
  87.0 244.1 %all-gather.15.cloned.1.call-start = ((), (), s32[]{:S(2)}) async-start(), calls=%async_computation.9 | async-start | bytes 5308416 | tf_op jit(solution)/shard_map/all_gather | solution.py:32
  281.9 137.3 %all-gather.9.cloned.1.call-start = ((), (), s32[]{:S(2)}) async-start(), calls=%async_computation.6 | async-start | bytes 10027008 | tf_op jit(solution)/shard_map/all_gather | solution.py:35
  292.2 1.1 copy-start.2
  292.3 212.0 %all-gather.17.cloned.1.call-start = ((), (), s32[]{:S(2)}) async-start(), calls=%async_computation.10 | async-start | bytes 10027008 | tf_op jit(solution)/shard_map/all_gather | solution.py:36
  295.8 133.2 %all-to-all-start.1 = ((bf16[8,768,384]{2,1,0:T(8,128)(2,1)}), bf16[8,768,384]{2,1,0:T(8,128)(2,1)}, u32[]{:S(2)}, u32[]{:S(2)}) async-start(bf16[8,768,384]{2,1,0:T(8,128)(2,1)} %stack.5), calls=%async_computation.1 | async-start | bytes 9437184 | tf_op jit(solution)/shard_map/all_to_all | solution.py:22
  429.0 75.3 %copy-start = (bf16[768,384]{1,0:T(8,128)(2,1)S(1)}, bf16[768,384]{1,0:T(8,128)(2,1)}, u32[]{:S(2)}) copy-start(bf16[768,384]{1,0:T(8,128)(2,1)} %fusion.9) | copy-start | bytes 1769476
Sparse Core Ops, SparseCore 0:
  78.5 71.4 all-gather.12
  152.2 33.8 all-gather.10
  188.2 83.8 all-gather.6
  282.1 49.0 all-gather.14
  333.7 85.4 all-gather.8
  421.2 83.0 all-gather.16
